TPU v7x, 32 devices: a whole 2x2x4 slice. The times are simulated.
32 devices in a mesh: prow: 8 (over z, x), pcol: 4 (over y, core).
Axes of the slice: x: 2, y: 2, z: 4, core: 2. Of those that a mesh axis runs over, the one named last changes fastest.
Arguments:
- matrix: bfloat16 [16384, 4096], P('prow', 'pcol'), may hold values from -6 to 6
- inverses: bfloat16 [2, 512, 512], replicated, may hold values from -0.01171875 to 0.01171875
Outputs:
- factored: bfloat16 [16384, 4096], P('prow', 'pcol')
All inputs are finite; a program needn't handle non-finite values.
Results may differ from a plain program's by a relative error of at most 0.0063.
Values may be sent and summed in bfloat16 or wider, within the bound.
A program may use at most 64 MiB of HBM per device.

v0:
```python
import jax
import jax.numpy as jnp
from jax import lax
from jax.sharding import PartitionSpec as P

STEPS = 2


def from_root(block, axis, holder):
    block = jnp.where(lax.axis_index(axis) == holder, block, jnp.zeros_like(block))
    return lax.psum(block, axis)


def per_device(matrix, inverses):
    my_row = lax.axis_index("prow")
    my_col = lax.axis_index("pcol")
    grid_rows = lax.axis_size("prow")
    grid_cols = lax.axis_size("pcol")
    block = inverses.shape[1]
    local_rows, local_cols = matrix.shape
    row_logical = jnp.arange(local_rows, dtype=jnp.int32) // block * grid_rows + my_row
    col_logical = jnp.arange(local_cols, dtype=jnp.int32) // block * grid_cols + my_col
    current = matrix.astype(jnp.float32)
    for step_index in range(STEPS):
        root_col = step_index % grid_cols
        col_start = step_index // grid_cols * block
        root_row = step_index % grid_rows
        row_start = step_index // grid_rows * block
        below = (row_logical > step_index)[:, None]
        right = (col_logical > step_index)[None, :]
        column = current[:, col_start : col_start + block]
        panel = column.astype(jnp.bfloat16)
        lower = jnp.dot(panel, inverses[step_index], preferred_element_type=jnp.float32).astype(
            jnp.bfloat16
        )
        lower = from_root(lower, "pcol", root_col)
        lower = jnp.where(below, lower, jnp.zeros_like(lower))
        upper = current[row_start : row_start + block, :].astype(jnp.bfloat16)
        upper = from_root(upper, "prow", root_row)
        upper = jnp.where(right, upper, jnp.zeros_like(upper))
        current = current - jnp.dot(lower, upper, preferred_element_type=jnp.float32)
        owner = jnp.logical_and(below, my_col == root_col)
        kept = current[:, col_start : col_start + block]
        current = current.at[:, col_start : col_start + block].set(
            jnp.where(owner, lower.astype(jnp.float32), kept)
        )
    return current.astype(jnp.bfloat16)


def solution(mesh):
    in_specs = (P("prow", "pcol"), P())
    out_specs = P("prow", "pcol")
    return jax.shard_map(
        per_device, mesh=mesh, in_specs=in_specs, out_specs=out_specs, check_vma=False
    )
```

profile of v0, /device:TPU:28, one launch (start us, length us, event | category | flops | bytes accessed | tf_op | source)
XLA Modules:
  0.0 317.1 jit_solution(1969258106479843967)
XLA Ops:
  6.5 0.0 all-reduce.5.cloned.1.call-start
  6.5 4.3 %fusion.1 = bf16[2048,512]{1,0:T(8,128)(2,1)} fusion(bf16[2048,1024]{1,0:T(8,128)(2,1)} %param.6, pred[]{:T(512)S(6)} %eq.14, bf16[2,512,512]{2,1,0:T(8,128)(2,1)} %param.7), kind=kOutput, calls=%fused_computation.7 | convolution fusion | flops 1075838976 | bytes 4718593 | tf_op jit(solution)/shard_map/dot_general | solution.py:33
  10.8 0.0 all-reduce.5.cloned.1.call-update
  10.8 0.0 all-reduce.7.cloned.1.call-start
  10.9 2.3 slice_select_fusion
  13.2 0.0 all-reduce.7.cloned.1.call-update
  13.2 0.0 all-reduce.11.cloned.1.call-start
  13.3 0.7 compare_reduce_fusion
  14.0 48.5 %all-reduce.5.cloned.1.call-done = bf16[2048,512]{1,0:T(8,128)(2,1)} async-done(((bf16[2048,512]{1,0:T(8,128)(2,1)}), bf16[2048,512]{1,0:T(8,128)(2,1)}) %all-reduce.5.cloned.1.call-update) | async-done | bytes 2097168 | tf_op jit(solution)/shard_map/psum | solution.py:11
  62.4 81.8 %all-reduce.7.cloned.1.call-done = bf16[512,1024]{1,0:T(8,128)(2,1)} async-done(((bf16[512,1024]{1,0:T(8,128)(2,1)}), bf16[512,1024]{1,0:T(8,128)(2,1)}) %all-reduce.7.cloned.1.call-update) | async-done | bytes 1048592 | tf_op jit(solution)/shard_map/psum | solution.py:11
  144.2 0.0 copy-start.1
  144.2 0.0 copy-start.3
  144.2 5.7 %convert_subtract_fusion = f32[2048,1024]{1,0:T(8,128)S(1)} fusion(bf16[2048,1024]{1,0:T(8,128)(2,1)} %param.6, bf16[512,1024]{1,0:T(8,128)(2,1)} %all-reduce.7.cloned.1.call-done, pred[1024]{0:T(1024)(128)(4,1)S(1)} %fusion.32, bf16[2048,512]{1,0:T(8,128)(2,1)} %all-reduce.5.cloned.1.call-done, pred[2048]{0:T(1024)(128)(4,1)S(1)} %get-tuple-element.31), kind=kOutput, calls=%fused_computation | convolution fusion | flops 2153250816 | bytes 15731712 | tf_op jit(solution)/shard_map/dot_general | solution.py:41
  149.9 0.0 copy-start
  150.0 3.2 %copy-done = f32[2048,1024]{1,0:T(8,128)} copy-done((f32[2048,1024]{1,0:T(8,128)}, f32[2048,1024]{1,0:T(8,128)S(1)}, u32[]{:S(2)}) %copy-start) | copy-done | bytes 8388632
  153.2 0.0 copy-done.1
  153.2 0.0 copy-done.3
  153.2 4.0 %fusion.2 = bf16[2048,512]{1,0:T(8,128)(2,1)} fusion(f32[2048,1024]{1,0:T(8,128)S(1)} %convert_subtract_fusion, pred[2048]{0:T(1024)(128)(4,1)S(1)} %get-tuple-element.32, pred[]{:T(512)S(6)} %eq.16, pred[]{:T(512)} %compare_reduce_fusion, bf16[2,512,512]{2,1,0:T(8,128)(2,1)S(1)} %copy-done.3, bf16[2048,512]{1,0:T(8,128)(2,1)S(1)} %copy-done.1, ...), kind=kOutput, calls=%fused_computation.8 | convolution fusion | flops 1080033280 | bytes 6819842 | tf_op jit(solution)/shard_map/dot_general | solution.py:33
  157.2 4.6 %fusion.4 = f32[2048,1024]{1,0:T(8,128)} fusion(f32[2048,1024]{1,0:T(8,128)} %copy-done, pred[2048]{0:T(1024)(128)(4,1)S(1)} %get-tuple-element.32, pred[]{:T(512)} %compare_reduce_fusion, bf16[2048,512]{1,0:T(8,128)(2,1)S(1)} %copy-done.1, pred[2048]{0:T(1024)(128)(4,1)S(1)} %get-tuple-element.31), kind=kLoop, calls=%fused_computation.10 | loop fusion | flops 4194304 | bytes 10490368 | tf_op jit(solution)/shard_map/scatter | solution.py:44
  161.8 2.7 fusion.9
  164.5 0.0 all-reduce.11.cloned.1.call-update
  164.5 0.0 all-reduce.9.cloned.1.call-start
  164.5 0.5 all-reduce.9.cloned.1.call-update
  165.1 77.1 %all-reduce.11.cloned.1.call-done = bf16[512,1024]{1,0:T(8,128)(2,1)} async-done(((bf16[512,1024]{1,0:T(8,128)(2,1)}), bf16[512,1024]{1,0:T(8,128)(2,1)}) %all-reduce.11.cloned.1.call-update) | async-done | bytes 1048592 | tf_op jit(solution)/shard_map/psum | solution.py:11
  242.2 53.6 %all-reduce.9.cloned.1.call-done = bf16[2048,512]{1,0:T(8,128)(2,1)} async-done(((bf16[2048,512]{1,0:T(8,128)(2,1)}), bf16[2048,512]{1,0:T(8,128)(2,1)}) %all-reduce.9.cloned.1.call-update) | async-done | bytes 2097168 | tf_op jit(solution)/shard_map/psum | solution.py:11
  295.8 0.0 copy-start.2
  295.8 8.9 %convolution_subtract_fusion = bf16[2048,1024]{1,0:T(8,128)(2,1)} fusion(f32[2048,1024]{1,0:T(8,128)} %fusion.4, bf16[512,1024]{1,0:T(8,128)(2,1)} %all-reduce.11.cloned.1.call-done, pred[1024]{0:T(1024)(128)(4,1)S(1)} %fusion.31, bf16[2048,512]{1,0:T(8,128)(2,1)} %all-reduce.9.cloned.1.call-done, pred[2048]{0:T(1024)(128)(4,1)S(1)} %get-tuple-element.29), kind=kOutput, calls=%fused_computation.4 | convolution fusion | flops 2153250816 | bytes 15731712 | tf_op jit(solution)/shard_map/dot_general | solution.py:41
  304.7 0.0 copy-done.2
  304.7 5.8 %fusion = bf16[2048,1024]{1,0:T(8,128)(2,1)} fusion(bf16[2048,1024]{1,0:T(8,128)(2,1)} %convolution_subtract_fusion, pred[2048]{0:T(1024)(128)(4,1)S(1)} %get-tuple-element.30, pred[]{:T(512)} %compare_reduce_fusion, bf16[2048,512]{1,0:T(8,128)(2,1)S(1)} %copy-done.2, pred[2048]{0:T(1024)(128)(4,1)S(1)} %get-tuple-element.29), kind=kLoop, calls=%fused_computation.3 | loop fusion | flops 4194304 | bytes 6296064 | tf_op jit(solution)/shard_map/scatter | solution.py:44
  (4 shorter events, 0.0 us)
Async XLA Ops:
  6.5 55.9 %all-reduce.5.cloned.1.call-start = ((), (), s32[]{:S(2)}) async-start(), calls=%async_computation | async-start | bytes 4194304 | tf_op jit(solution)/shard_map/psum | solution.py:11
  10.8 133.4 %all-reduce.7.cloned.1.call-start = ((), (), s32[]{:S(2)}) async-start(), calls=%async_computation.1 | async-start | bytes 2097152 | tf_op jit(solution)/shard_map/psum | solution.py:11
  13.2 229.0 %all-reduce.11.cloned.1.call-start = ((), (), s32[]{:S(2)}) async-start(), calls=%async_computation.3 | async-start | bytes 2097152 | tf_op jit(solution)/shard_map/psum | solution.py:11
  144.2 8.9 %copy-start.1 = (bf16[2048,512]{1,0:T(8,128)(2,1)S(1)}, bf16[2048,512]{1,0:T(8,128)(2,1)}, u32[]{:S(2)}) copy-start(bf16[2048,512]{1,0:T(8,128)(2,1)} %all-reduce.5.cloned.1.call-done) | copy-start | bytes 6291460
  144.2 8.9 %copy-start.3 = (bf16[2,512,512]{2,1,0:T(8,128)(2,1)S(1)}, bf16[2,512,512]{2,1,0:T(8,128)(2,1)}, u32[]{:S(2)}) copy-start(bf16[2,512,512]{2,1,0:T(8,128)(2,1)} %param.7) | copy-start | bytes 3145732
  149.9 3.2 %copy-start = (f32[2048,1024]{1,0:T(8,128)}, f32[2048,1024]{1,0:T(8,128)S(1)}, u32[]{:S(2)}) copy-start(f32[2048,1024]{1,0:T(8,128)S(1)} %convert_subtract_fusion) | copy-start | bytes 25165828
  164.5 131.3 %all-reduce.9.cloned.1.call-start = ((), (), s32[]{:S(2)}) async-start(), calls=%async_computation.2 | async-start | bytes 4194304 | tf_op jit(solution)/shard_map/psum | solution.py:11
  295.8 8.9 %copy-start.2 = (bf16[2048,512]{1,0:T(8,128)(2,1)S(1)}, bf16[2048,512]{1,0:T(8,128)(2,1)}, u32[]{:S(2)}) copy-start(bf16[2048,512]{1,0:T(8,128)(2,1)} %all-reduce.9.cloned.1.call-done) | copy-start | bytes 6291460
Sparse Core Ops, SparseCore 0:
  10.9 51.4 all-reduce.4
  66.4 77.8 all-reduce.6
  164.6 77.5 all-reduce.10
  244.6 51.2 all-reduce.8
where the time goes:
time: 320 us; the launch traced here: 317 us
  waiting for transfers between devices  262 us (82%)
  matrix products  22.8 us (7%)
  other arithmetic  16.1 us (5%)
  between operations  13.2 us (4%)
  local copies, waits for them, and re-layouts  3.22 us (1%)
    psum x4, waiting for transfers between devices, from_root(): return lax.psum(block, axis)  261 us
    dot_general x2, matrix products, per_device(): jnp.dot(lower, upper, preferred_element_type=jnp.float32)  14.6 us
    scatter x2, other arithmetic, per_device(): current.at[:, col_start:col_start + block]  10.4 us
    dot_general x2, matrix products, per_device(): jnp.dot(panel, inverses[step_index], preferred_element_type=jnp.float32)  8.24 us
  transfers between devices with their start and end apart: 4, of which 4 were waited for; matrix products, arithmetic and copies ran while one was open for 1% of the time, Pallas kernels for 0%

commit v1 on v0

v1 whole, which is shorter than its diff:
```python
import functools

import jax
import jax.numpy as jnp
from jax import lax
from jax.experimental import pallas as pl
from jax.experimental.pallas import tpu as pltpu
from jax.sharding import PartitionSpec as P

MESH = pl.DeviceIdType.MESH
ROW_CHUNK = 256
COL_CHUNK = 128
U01_PARTS = 2


def kernel(
    n_rows, n_cols, m, inv, out,
    cur, res, pan, low, u, u01, ivm,
    load_sem, inv_sem, out_sem,
    y_send, y_recv, s_send, s_recv,
    z_send, z_recv, x_send, x_recv,
    c_send, cz_send, cx_send, cs_send, c_recv,
):
    p = lax.axis_index("prow")
    q = lax.axis_index("pcol")
    chip, core = q // 2, q % 2
    chips = n_cols // 2
    par = p % 2
    block = inv.shape[1]
    rows_dev, cols_dev = m.shape
    ny = rows_dev // ROW_CHUNK
    nb = block // ROW_CHUNK
    nu = cols_dev // COL_CHUNK
    part = block // U01_PARTS
    sib = q + 1 - 2 * core
    mate = p + 1 - 2 * par
    origin = jnp.logical_and(p == 0, q == 1)

    def rows_of(j):
        return pl.ds(pl.multiple_of(j * ROW_CHUNK, ROW_CHUNK), ROW_CHUNK)

    def cols_of(n):
        return pl.ds(pl.multiple_of(n * COL_CHUNK, COL_CHUNK), COL_CHUNK)

    def part_of(i):
        return pl.ds(i * part, part)

    def need(k, j):
        return jnp.logical_or(j * ROW_CHUNK >= block, p > k)

    def when(*conds):
        return pl.when(functools.reduce(jnp.logical_and, conds))

    def wait(ref, sem):
        pltpu.make_async_copy(ref, ref, sem).wait()

    def send(ref, send_sem, recv_sem, to):
        pltpu.make_async_remote_copy(
            src_ref=ref, dst_ref=ref, send_sem=send_sem, recv_sem=recv_sem,
            device_id=to, device_id_type=MESH,
        ).start()

    def u_ref(h, n):
        return u.at[pl.ds(pl.multiple_of(h * block, block), block), cols_of(n)]

    @when(p == 0)
    def _():
        @pl.loop(0, nu)
        def _(n):
            pltpu.make_async_copy(
                m.at[pl.ds(0, block), cols_of(n)], u_ref(0, n), z_recv.at[n]
            ).start()

    @when(origin)
    def _():
        for i in range(U01_PARTS):
            pltpu.make_async_copy(
                m.at[pl.ds(0, block), part_of(i)], u01.at[:, part_of(i)], c_recv.at[i]
            ).start()

    @when(chip == 0)
    def _():
        @pl.loop(0, ny)
        def _(j):
            @when(need(core, j))
            def _():
                pltpu.make_async_copy(
                    m.at[rows_of(j), pl.ds(0, block)], pan.at[core, rows_of(j)], y_recv.at[j]
                ).start()

    pltpu.make_async_copy(inv, ivm, inv_sem).start()
    pltpu.make_async_copy(m, cur, load_sem).start()

    barrier = pltpu.get_barrier_semaphore()

    def greet(to):
        pl.semaphore_signal(barrier, inc=1, device_id=to, device_id_type=MESH)

    greet((p, sib))
    greet((mate, q))
    up, down = chip + 1 < chips, chip > 0
    ahead, behind = p + 2 < n_rows, p >= 2

    @when(up)
    def _():
        greet((p, q + 2))

    @when(down)
    def _():
        greet((p, q - 2))

    @when(ahead)
    def _():
        greet((p + 2, q))

    @when(behind)
    def _():
        greet((p - 2, q))

    count = 2
    for cond in (up, down, ahead, behind):
        count = count + cond.astype(jnp.int32)
    pl.semaphore_wait(barrier, count)

    def panel_step(j):
        @when(need(core, j))
        def _():
            mine = pan.at[core, rows_of(j)]
            wait(mine, y_recv.at[j])

            @when(up)
            def _():
                send(mine, y_send.at[j], y_recv.at[j], (p, q + 2))

            send(mine, s_send.at[j], s_recv.at[j], (p, sib))

    def lower0(j):
        rows = rows_of(j)

        @when(need(0, j), core == 1)
        def _():
            wait(pan.at[0, rows], s_recv.at[j])

        @when(need(0, j))
        def _():
            low[rows, :block] = jnp.dot(
                pan[0, rows, :], ivm[0], preferred_element_type=jnp.float32
            ).astype(low.dtype)

        @when(jnp.logical_not(need(0, j)))
        def _():
            low[rows, :block] = jnp.zeros((ROW_CHUNK, block), low.dtype)

    def lower1(j):
        rows = rows_of(j)

        @when(need(1, j), core == 0)
        def _():
            wait(pan.at[1, rows], s_recv.at[j])

        @when(need(1, j))
        def _():
            panel = (
                pan[1, rows, :].astype(jnp.float32)
                - jnp.dot(low[rows, :block], u01[...], preferred_element_type=jnp.float32)
            ).astype(low.dtype)
            low[rows, block:] = jnp.dot(
                panel, ivm[1], preferred_element_type=jnp.float32
            ).astype(low.dtype)

        @when(jnp.logical_not(need(1, j)))
        def _():
            low[rows, block:] = jnp.zeros((ROW_CHUNK, block), low.dtype)

    def update(j):
        rows = rows_of(j)

        def plain(b):
            cols = slice(b * block, (b + 1) * block)
            res[rows, cols] = (
                cur[rows, cols].astype(jnp.float32)
                - jnp.dot(low[rows, :], u[:, cols], preferred_element_type=jnp.float32)
            ).astype(res.dtype)

        for k in range(2):
            @when(q == k, need(k, j))
            def _(k=k):
                res[rows, :block] = low[rows, k * block : (k + 1) * block]

        @when(jnp.logical_not(jnp.logical_and(chip == 0, need(core, j))))
        def _():
            plain(0)

        for b in range(1, cols_dev // block):
            plain(b)
        pltpu.make_async_copy(res.at[rows], out.at[rows], out_sem.at[j]).start()

    def u_step(n):
        @when(p == 1)
        def _():
            wait(u_ref(0, n), x_recv.at[n])
            cols = cols_of(n)
            u[block:, cols] = (
                cur[:block, cols].astype(jnp.float32)
                - jnp.dot(low[:block, :block], u[:block, cols], preferred_element_type=jnp.float32)
            ).astype(u.dtype)

        @when(p != 1)
        def _():
            wait(u_ref(par, n), z_recv.at[n])

        @when(ahead)
        def _():
            send(u_ref(par, n), z_send.at[n], z_recv.at[n], (p + 2, q))

        send(u_ref(par, n), x_send.at[n], x_recv.at[n], (mate, q))

    def u01_right(i):
        @when(p == 0, up)
        def _():
            send(u01.at[:, part_of(i)], c_send.at[i], c_recv.at[i], (p, q + 2))

    @when(origin)
    def _():
        for i in range(U01_PARTS):
            wait(u01.at[:, part_of(i)], c_recv.at[i])
            u01_right(i)

    @when(p == 0)
    def _():
        @pl.loop(0, nu)
        def _(n):
            u_step(n)

    @when(jnp.logical_or(chip == 0, p == 1))
    def _():
        @pl.loop(0, nb)
        def _(j):
            panel_step(j)

    wait(ivm, inv_sem)
    wait(cur, load_sem)

    early = 2

    @when(p == 1)
    def _():
        @pl.loop(0, nb)
        def _(j):
            lower0(j)

        @pl.loop(0, early)
        def _(n):
            u_step(n)

    @when(chip == 0)
    def _():
        @pl.loop(nb, ny)
        def _(j):
            panel_step(j)

    def later_panel(j):
        @when(chip > 0, jnp.logical_or(p != 1, j >= nb))
        def _():
            panel_step(j)

    @when(p > 0)
    def _():
        @pl.loop(jnp.where(p == 1, early, 0), nu)
        def _(n):
            u_step(n)

    @when(core == 1)
    def _():
        for i in range(U01_PARTS):
            mine = u01.at[:, part_of(i)]

            @when(jnp.logical_not(origin))
            def _():
                wait(mine, c_recv.at[i])
                u01_right(i)

            send(mine, cs_send.at[i], c_recv.at[i], (p, sib))

            @when(par == 0)
            def _():
                @when(ahead)
                def _():
                    send(mine, cz_send.at[i], c_recv.at[i], (p + 2, q))

                send(mine, cx_send.at[i], c_recv.at[i], (mate, q))

    @when(core == 0)
    def _():
        for i in range(U01_PARTS):
            wait(u01.at[:, part_of(i)], c_recv.at[i])

    @when(p != 1)
    def _():
        @pl.loop(0, nu)
        def _(n):
            wait(u_ref(1 - par, n), x_recv.at[n])

    @pl.loop(0, ny)
    def _(j):
        later_panel(j)

        @when(jnp.logical_or(p != 1, j >= nb))
        def _():
            lower0(j)

        lower1(j)
        update(j)

    @pl.loop(0, ny)
    def _(j):
        wait(res.at[rows_of(j)], out_sem.at[j])

        @when(need(core, j))
        def _():
            mine = pan.at[core, rows_of(j)]
            wait(mine, s_send.at[j])

            @when(up)
            def _():
                wait(mine, y_send.at[j])

    @pl.loop(0, nu)
    def _(n):
        wait(u_ref(par, n), x_send.at[n])

        @when(ahead)
        def _():
            wait(u_ref(par, n), z_send.at[n])

    @when(core == 1)
    def _():
        for i in range(U01_PARTS):
            mine = u01.at[:, part_of(i)]
            wait(mine, cs_send.at[i])

            @when(p == 0, up)
            def _():
                wait(mine, c_send.at[i])

            @when(par == 0)
            def _():
                wait(mine, cx_send.at[i])

                @when(ahead)
                def _():
                    wait(mine, cz_send.at[i])


def per_device(n_rows, n_cols, matrix, inverses):
    rows_dev, cols_dev = matrix.shape
    block = inverses.shape[1]
    kind = matrix.dtype
    ny, nu = rows_dev // ROW_CHUNK, cols_dev // COL_CHUNK
    dma = pltpu.SemaphoreType.DMA
    return pl.pallas_call(
        functools.partial(kernel, n_rows, n_cols),
        out_shape=jax.ShapeDtypeStruct(matrix.shape, kind),
        in_specs=[pl.BlockSpec(memory_space=pl.ANY)] * 2,
        out_specs=pl.BlockSpec(memory_space=pl.ANY),
        scratch_shapes=[
            pltpu.VMEM((rows_dev, cols_dev), kind),
            pltpu.VMEM((rows_dev, cols_dev), kind),
            pltpu.VMEM((2, rows_dev, block), kind),
            pltpu.VMEM((rows_dev, 2 * block), kind),
            pltpu.VMEM((2 * block, cols_dev), kind),
            pltpu.VMEM((block, block), kind),
            pltpu.VMEM(inverses.shape, kind),
            dma, dma, dma((ny,)),
            dma((ny,)), dma((ny,)), dma((ny,)), dma((ny,)),
            dma((nu,)), dma((nu,)), dma((nu,)), dma((nu,)),
            dma((U01_PARTS,)), dma((U01_PARTS,)), dma((U01_PARTS,)), dma((U01_PARTS,)),
            dma((U01_PARTS,)),
        ],
        compiler_params=pltpu.CompilerParams(
            collective_id=0, has_side_effects=True, vmem_limit_bytes=44 * 2**20
        ),
    )(matrix, inverses)


def solution(mesh):
    body = functools.partial(per_device, mesh.shape["prow"], mesh.shape["pcol"])
    return jax.shard_map(
        body, mesh=mesh, in_specs=(P("prow", "pcol"), P()),
        out_specs=P("prow", "pcol"), check_vma=False,
    )
```

time: 320 us -> 78.8 us (0.25)
  waiting for transfers between devices: 262 us -> 0 us
  Pallas kernels: 0 us -> 73.2 us
  matrix products: 22.8 us -> 0 us
  other arithmetic: 16.1 us -> 0 us
  between operations: 13.2 us -> 0.01 us
    psum x4 -> x0, waiting for transfers between devices: 261 us -> none  [from_root(): return lax.psum(block, axis)]
    pallas_call x0 -> x1, Pallas kernels: none -> 73.2 us  [per_device(): pl.pallas_call(functools.partial(kernel, n_rows, n_cols), out_shape=jax.S...]
    dot_general x4 -> x0, matrix products: 22.8 us -> none  [the longest x2 14.6 us: per_device(): jnp.dot(lower, upper, preferred_element_type=jnp.float32)]
    scatter x2 -> x0, other arithmetic: 10.4 us -> none  [per_device(): current.at[:, col_start:col_start + block]]
    select_n x2 -> x0, other arithmetic: 4.99 us -> none  [from_root(): jnp.where(lax.axis_index(axis) == holder, block, jnp.zeros_like(block))]
  transfers between devices with their start and end apart: 4 -> 0, of which waited for: 4 -> 0; matrix products, arithmetic and copies ran while one was open for 1% -> 0% of each run, Pallas kernels for 0% -> 0%
where the time goes in v1:
time: 78.8 us; the launch traced here: 78.7 us
  Pallas kernels  73.2 us (93%)
  local copies, waits for them, and re-layouts  5.43 us (7%)
    pallas_call x1, Pallas kernels, per_device(): pl.pallas_call(functools.partial(kernel, n_rows, n_cols), out_shape=jax.S...  73.2 us
    unnamed x5, local copies, waits for them, and re-layouts  5.43 us

profile of v1, /device:TPU:28, one launch (start us, length us, event | category | flops | bytes accessed | tf_op | source)
XLA Modules:
  0.0 78.7 jit_solution(16708703288494068426)
XLA Ops:
  0.0 0.0 copy-start
  0.0 2.2 %copy-done = bf16[2048,1024]{1,0:T(8,128)(2,1)S(1)} copy-done((bf16[2048,1024]{1,0:T(8,128)(2,1)S(1)}, bf16[2048,1024]{1,0:T(8,128)(2,1)}, u32[]{:S(2)}) %copy-start) | copy-done | bytes 4194328
  2.2 0.0 copy-start.1
  2.2 1.2 %copy-done.1 = bf16[2,512,512]{2,1,0:T(8,128)(2,1)S(1)} copy-done((bf16[2,512,512]{2,1,0:T(8,128)(2,1)S(1)}, bf16[2,512,512]{2,1,0:T(8,128)(2,1)}, u32[]{:S(2)}) %copy-start.1) | copy-done | bytes 1048600
  3.4 73.2 %shard_map.28 = bf16[2048,1024]{1,0:T(8,128)(2,1)S(1)} custom-call(bf16[2048,1024]{1,0:T(8,128)(2,1)S(1)} %copy-done, bf16[2,512,512]{2,1,0:T(8,128)(2,1)S(1)} %copy-done.1), custom_call_target="tpu_custom_call" | custom-call | tf_op jit(solution)/shard_map/pallas_call | solution.py:361
  76.6 2.0 %copy.4 = bf16[2048,1024]{1,0:T(8,128)(2,1)} copy(bf16[2048,1024]{1,0:T(8,128)(2,1)S(1)} %shard_map.28) | data formatting | bytes 8388608
Async XLA Ops:
  0.0 2.2 %copy-start = (bf16[2048,1024]{1,0:T(8,128)(2,1)S(1)}, bf16[2048,1024]{1,0:T(8,128)(2,1)}, u32[]{:S(2)}) copy-start(bf16[2048,1024]{1,0:T(8,128)(2,1)} %m.1) | copy-start | bytes 12582916
  2.2 1.2 %copy-start.1 = (bf16[2,512,512]{2,1,0:T(8,128)(2,1)S(1)}, bf16[2,512,512]{2,1,0:T(8,128)(2,1)}, u32[]{:S(2)}) copy-start(bf16[2,512,512]{2,1,0:T(8,128)(2,1)} %inv.1) | copy-start | bytes 3145732

commit v2 on v1

--- a/solution.py
+++ b/solution.py
@@ -8,7 +8,11 @@
 from jax.sharding import PartitionSpec as P
 
 MESH = pl.DeviceIdType.MESH
-ROW_CHUNK = 256
+ROW_CHUNK = 512
+SEND_ROWS = 128
+WINDOW = 6
+HELD_BACK = 2
+U01_AT = 8
 COL_CHUNK = 128
 U01_PARTS = 2
 
@@ -28,8 +32,10 @@
     par = p % 2
     block = inv.shape[1]
     rows_dev, cols_dev = m.shape
-    ny = rows_dev // ROW_CHUNK
-    nb = block // ROW_CHUNK
+    ny = rows_dev // SEND_ROWS
+    nb = block // SEND_ROWS
+    nr = rows_dev // ROW_CHUNK
+    per = ROW_CHUNK // SEND_ROWS
     nu = cols_dev // COL_CHUNK
     part = block // U01_PARTS
     sib = q + 1 - 2 * core
@@ -39,6 +45,9 @@
     def rows_of(j):
         return pl.ds(pl.multiple_of(j * ROW_CHUNK, ROW_CHUNK), ROW_CHUNK)
 
+    def sent_rows(j):
+        return pl.ds(pl.multiple_of(j * SEND_ROWS, SEND_ROWS), SEND_ROWS)
+
     def cols_of(n):
         return pl.ds(pl.multiple_of(n * COL_CHUNK, COL_CHUNK), COL_CHUNK)
 
@@ -47,6 +56,9 @@
 
     def need(k, j):
         return jnp.logical_or(j * ROW_CHUNK >= block, p > k)
+
+    def sent(k, j):
+        return jnp.logical_or(j * SEND_ROWS >= block, p > k)
 
     def when(*conds):
         return pl.when(functools.reduce(jnp.logical_and, conds))
@@ -82,10 +94,10 @@
     def _():
         @pl.loop(0, ny)
         def _(j):
-            @when(need(core, j))
+            @when(sent(core, j))
             def _():
                 pltpu.make_async_copy(
-                    m.at[rows_of(j), pl.ds(0, block)], pan.at[core, rows_of(j)], y_recv.at[j]
+                    m.at[sent_rows(j), pl.ds(0, block)], pan.at[core, sent_rows(j)], y_recv.at[j]
                 ).start()
 
     pltpu.make_async_copy(inv, ivm, inv_sem).start()
@@ -123,9 +135,13 @@
     pl.semaphore_wait(barrier, count)
 
     def panel_step(j):
-        @when(need(core, j))
-        def _():
-            mine = pan.at[core, rows_of(j)]
+        @when(up, j >= WINDOW, sent(core, j - WINDOW))
+        def _():
+            wait(pan.at[core, sent_rows(j - WINDOW)], y_send.at[j - WINDOW])
+
+        @when(sent(core, j))
+        def _():
+            mine = pan.at[core, sent_rows(j)]
             wait(mine, y_recv.at[j])
 
             @when(up)
@@ -139,7 +155,8 @@
 
         @when(need(0, j), core == 1)
         def _():
-            wait(pan.at[0, rows], s_recv.at[j])
+            for i in range(per):
+                wait(pan.at[0, sent_rows(j * per + i)], s_recv.at[j * per + i])
 
         @when(need(0, j))
         def _():
@@ -156,7 +173,8 @@
 
         @when(need(1, j), core == 0)
         def _():
-            wait(pan.at[1, rows], s_recv.at[j])
+            for i in range(per):
+                wait(pan.at[1, sent_rows(j * per + i)], s_recv.at[j * per + i])
 
         @when(need(1, j))
         def _():
@@ -175,8 +193,8 @@
     def update(j):
         rows = rows_of(j)
 
-        def plain(b):
-            cols = slice(b * block, (b + 1) * block)
+        def plain(first, last):
+            cols = slice(first, last)
             res[rows, cols] = (
                 cur[rows, cols].astype(jnp.float32)
                 - jnp.dot(low[rows, :], u[:, cols], preferred_element_type=jnp.float32)
@@ -187,12 +205,16 @@
             def _(k=k):
                 res[rows, :block] = low[rows, k * block : (k + 1) * block]
 
-        @when(jnp.logical_not(jnp.logical_and(chip == 0, need(core, j))))
-        def _():
-            plain(0)
-
-        for b in range(1, cols_dev // block):
-            plain(b)
+        special = jnp.logical_and(chip == 0, need(core, j))
+
+        @when(jnp.logical_not(special))
+        def _():
+            plain(0, cols_dev)
+
+        @when(special)
+        def _():
+            plain(block, cols_dev)
+
         pltpu.make_async_copy(res.at[rows], out.at[rows], out_sem.at[j]).start()
 
     def u_step(n):
@@ -220,80 +242,107 @@
         def _():
             send(u01.at[:, part_of(i)], c_send.at[i], c_recv.at[i], (p, q + 2))
 
+    def u01_step(i):
+        mine = u01.at[:, part_of(i)]
+
+        @when(jnp.logical_not(origin))
+        def _():
+            wait(mine, c_recv.at[i])
+
+        @when(core == 1)
+        def _():
+            @when(jnp.logical_not(origin))
+            def _():
+                u01_right(i)
+
+            send(mine, cs_send.at[i], c_recv.at[i], (p, sib))
+
+            @when(par == 0)
+            def _():
+                @when(ahead)
+                def _():
+                    send(mine, cz_send.at[i], c_recv.at[i], (p + 2, q))
+
+                send(mine, cx_send.at[i], c_recv.at[i], (mate, q))
+
+    def prow_step(n):
+        for i in range(U01_PARTS):
+            @when(n == U01_AT + i)
+            def _(i=i):
+                u01_step(i)
+
+        @when(n < U01_AT)
+        def _():
+            u_step(n)
+
+        @when(n >= U01_AT + U01_PARTS)
+        def _():
+            u_step(n - U01_PARTS)
+
+    prow_steps = nu + U01_PARTS
+
     @when(origin)
     def _():
         for i in range(U01_PARTS):
             wait(u01.at[:, part_of(i)], c_recv.at[i])
             u01_right(i)
 
+    ahead_of = 2
+
     @when(p == 0)
     def _():
-        @pl.loop(0, nu)
+        @pl.loop(0, ahead_of)
         def _(n):
-            u_step(n)
-
-    @when(jnp.logical_or(chip == 0, p == 1))
+            prow_step(n)
+
+    wait(ivm, inv_sem)
+
+    @when(p == 1)
     def _():
         @pl.loop(0, nb)
         def _(j):
             panel_step(j)
 
-    wait(ivm, inv_sem)
-    wait(cur, load_sem)
-
-    early = 2
-
-    @when(p == 1)
-    def _():
-        @pl.loop(0, nb)
+        @pl.loop(0, nb // per)
         def _(j):
             lower0(j)
 
-        @pl.loop(0, early)
+        wait(cur, load_sem)
+
+        @pl.loop(0, ahead_of)
         def _(n):
-            u_step(n)
-
-    @when(chip == 0)
-    def _():
-        @pl.loop(nb, ny)
-        def _(j):
-            panel_step(j)
-
-    def later_panel(j):
-        @when(chip > 0, jnp.logical_or(p != 1, j >= nb))
-        def _():
-            panel_step(j)
-
-    @when(p > 0)
-    def _():
-        @pl.loop(jnp.where(p == 1, early, 0), nu)
-        def _(n):
-            u_step(n)
-
-    @when(core == 1)
-    def _():
-        for i in range(U01_PARTS):
-            mine = u01.at[:, part_of(i)]
-
-            @when(jnp.logical_not(origin))
-            def _():
-                wait(mine, c_recv.at[i])
-                u01_right(i)
-
-            send(mine, cs_send.at[i], c_recv.at[i], (p, sib))
-
-            @when(par == 0)
-            def _():
-                @when(ahead)
-                def _():
-                    send(mine, cz_send.at[i], c_recv.at[i], (p + 2, q))
-
-                send(mine, cx_send.at[i], c_recv.at[i], (mate, q))
-
-    @when(core == 0)
-    def _():
-        for i in range(U01_PARTS):
-            wait(u01.at[:, part_of(i)], c_recv.at[i])
+            prow_step(n)
+
+    @when(p != 1)
+    def _():
+        wait(cur, load_sem)
+
+    hops = p // 2 + par
+    lag = jnp.where(chip == 0, WINDOW, 0)
+    offset = jnp.where(p == 0, ahead_of, 1 - hops - lag)
+    slots = jnp.where(chip == 0, ny, ny - HELD_BACK)
+
+    @pl.loop(0, slots)
+    def _(t):
+        @when(jnp.logical_or(p != 1, t >= nb))
+        def _():
+            panel_step(t)
+
+        n = t + offset
+
+        @when(n >= jnp.where(p <= 1, ahead_of, 0), n < prow_steps)
+        def _():
+            prow_step(n)
+
+        j = t // per - 1
+
+        @when(t % per == per - 1, j >= jnp.where(p == 1, nb // per, 0))
+        def _():
+            lower0(j)
+
+    @pl.loop(jnp.clip(slots + offset, 0, prow_steps), prow_steps)
+    def _(n):
+        prow_step(n)
 
     @when(p != 1)
     def _():
@@ -301,27 +350,35 @@
         def _(n):
             wait(u_ref(1 - par, n), x_recv.at[n])
 
+    lowered = slots // per - 1
+
+    @pl.loop(0, nr)
+    def _(j):
+        t = slots + j - (nr - 1 - HELD_BACK)
+
+        @when(t >= slots, t < ny)
+        def _():
+            panel_step(t)
+
+        @when(j >= lowered)
+        def _():
+            lower0(j)
+
+        lower1(j)
+        update(j)
+
+    @pl.loop(0, nr)
+    def _(j):
+        wait(res.at[rows_of(j)], out_sem.at[j])
+
     @pl.loop(0, ny)
     def _(j):
-        later_panel(j)
-
-        @when(jnp.logical_or(p != 1, j >= nb))
-        def _():
-            lower0(j)
-
-        lower1(j)
-        update(j)
-
-    @pl.loop(0, ny)
-    def _(j):
-        wait(res.at[rows_of(j)], out_sem.at[j])
-
-        @when(need(core, j))
-        def _():
-            mine = pan.at[core, rows_of(j)]
+        @when(sent(core, j))
+        def _():
+            mine = pan.at[core, sent_rows(j)]
             wait(mine, s_send.at[j])
 
-            @when(up)
+            @when(up, j >= ny - WINDOW)
             def _():
                 wait(mine, y_send.at[j])
 
@@ -356,7 +413,7 @@
     rows_dev, cols_dev = matrix.shape
     block = inverses.shape[1]
     kind = matrix.dtype
-    ny, nu = rows_dev // ROW_CHUNK, cols_dev // COL_CHUNK
+    ny, nu, nr = rows_dev // SEND_ROWS, cols_dev // COL_CHUNK, rows_dev // ROW_CHUNK
     dma = pltpu.SemaphoreType.DMA
     return pl.pallas_call(
         functools.partial(kernel, n_rows, n_cols),
@@ -371,14 +428,14 @@
             pltpu.VMEM((2 * block, cols_dev), kind),
             pltpu.VMEM((block, block), kind),
             pltpu.VMEM(inverses.shape, kind),
-            dma, dma, dma((ny,)),
+            dma, dma, dma((nr,)),
             dma((ny,)), dma((ny,)), dma((ny,)), dma((ny,)),
             dma((nu,)), dma((nu,)), dma((nu,)), dma((nu,)),
             dma((U01_PARTS,)), dma((U01_PARTS,)), dma((U01_PARTS,)), dma((U01_PARTS,)),
             dma((U01_PARTS,)),
         ],
         compiler_params=pltpu.CompilerParams(
-            collective_id=0, has_side_effects=True, vmem_limit_bytes=44 * 2**20
+            collective_id=0, has_side_effects=True, vmem_limit_bytes=60 * 2**20
         ),
     )(matrix, inverses)
 

time: 78.8 us -> 64.9 us (0.82)
  Pallas kernels: 73.2 us -> 60.1 us
  local copies, waits for them, and re-layouts: 5.43 us -> 4.64 us
    pallas_call x1, Pallas kernels: 73.2 us -> 60.1 us  [per_device(): pl.pallas_call(functools.partial(kernel, n_rows, n_cols), out_shape=jax.S...]
    unnamed x5 -> x1, local copies, waits for them, and re-layouts: 5.43 us -> 4.64 us
where the time goes in v2:
time: 64.9 us; the launch traced here: 64.7 us
  Pallas kernels  60.1 us (93%)
  local copies, waits for them, and re-layouts  4.64 us (7%)
    pallas_call x1, Pallas kernels, per_device(): pl.pallas_call(functools.partial(kernel, n_rows, n_cols), out_shape=jax.S...  60.1 us
    unnamed x1, local copies, waits for them, and re-layouts  4.64 us

profile of v2, /device:TPU:28, one launch (start us, length us, event | category | flops | bytes accessed | tf_op | source)
XLA Modules:
  0.0 64.7 jit_solution(8456290030376137929)
XLA Ops:
  0.0 60.1 %shard_map.28 = bf16[2048,1024]{1,0:T(8,128)(2,1)} custom-call(bf16[2048,1024]{1,0:T(8,128)(2,1)} %m.1, bf16[2,512,512]{2,1,0:T(8,128)(2,1)} %inv.1), custom_call_target="tpu_custom_call" | custom-call | tf_op jit(solution)/shard_map/pallas_call | solution.py:418
  60.1 4.6 %copy.4 = bf16[2048,1024]{1,0:T(8,128)(2,1)} copy(bf16[2048,1024]{1,0:T(8,128)(2,1)} %shard_map.28) | data formatting | bytes 8388608

commit v3 on v2

--- a/solution.py
+++ b/solution.py
@@ -9,12 +9,13 @@
 
 MESH = pl.DeviceIdType.MESH
 ROW_CHUNK = 512
-SEND_ROWS = 128
-WINDOW = 6
-HELD_BACK = 2
-U01_AT = 8
+SEND_ROWS = 64
+WINDOW = 12
+HELD_BACK = 4
+U01_AT = 16
 COL_CHUNK = 128
-U01_PARTS = 2
+U01_PARTS = 4
+U_HALVES = 2
 
 
 def kernel(
@@ -36,7 +37,8 @@
     nb = block // SEND_ROWS
     nr = rows_dev // ROW_CHUNK
     per = ROW_CHUNK // SEND_ROWS
-    nu = cols_dev // COL_CHUNK
+    nu = U_HALVES * (cols_dev // COL_CHUNK)
+    half = block // U_HALVES
     part = block // U01_PARTS
     sib = q + 1 - 2 * core
     mate = p + 1 - 2 * par
@@ -73,14 +75,20 @@
         ).start()
 
     def u_ref(h, n):
-        return u.at[pl.ds(pl.multiple_of(h * block, block), block), cols_of(n)]
+        first = h * block + n % U_HALVES * half
+        return u.at[pl.ds(pl.multiple_of(first, half), half), cols_of(n // U_HALVES)]
 
     @when(p == 0)
     def _():
         @pl.loop(0, nu)
         def _(n):
             pltpu.make_async_copy(
-                m.at[pl.ds(0, block), cols_of(n)], u_ref(0, n), z_recv.at[n]
+                m.at[
+                    pl.ds(pl.multiple_of(n % U_HALVES * half, half), half),
+                    cols_of(n // U_HALVES),
+                ],
+                u_ref(0, n),
+                z_recv.at[n],
             ).start()
 
     @when(origin)
@@ -218,10 +226,11 @@
         pltpu.make_async_copy(res.at[rows], out.at[rows], out_sem.at[j]).start()
 
     def u_step(n):
-        @when(p == 1)
-        def _():
-            wait(u_ref(0, n), x_recv.at[n])
-            cols = cols_of(n)
+        @when(p == 1, n % U_HALVES == 0)
+        def _():
+            for i in range(U_HALVES):
+                wait(u_ref(0, n + i), x_recv.at[n + i])
+            cols = cols_of(n // U_HALVES)
             u[block:, cols] = (
                 cur[:block, cols].astype(jnp.float32)
                 - jnp.dot(low[:block, :block], u[:block, cols], preferred_element_type=jnp.float32)
@@ -287,7 +296,7 @@
             wait(u01.at[:, part_of(i)], c_recv.at[i])
             u01_right(i)
 
-    ahead_of = 2
+    ahead_of = 4
 
     @when(p == 0)
     def _():
@@ -319,8 +328,8 @@
 
     hops = p // 2 + par
     lag = jnp.where(chip == 0, WINDOW, 0)
-    offset = jnp.where(p == 0, ahead_of, 1 - hops - lag)
-    slots = jnp.where(chip == 0, ny, ny - HELD_BACK)
+    offset = jnp.where(p == 0, ahead_of, 1 - 2 * hops - lag)
+    slots = jnp.where(chip == 0, ny, jnp.minimum(ny - HELD_BACK, prow_steps + 2 * hops))
 
     @pl.loop(0, slots)
     def _(t):
@@ -354,10 +363,8 @@
 
     @pl.loop(0, nr)
     def _(j):
-        t = slots + j - (nr - 1 - HELD_BACK)
-
-        @when(t >= slots, t < ny)
-        def _():
+        @pl.loop(jnp.maximum(slots, per * j), jnp.maximum(slots, per * (j + 1)))
+        def _(t):
             panel_step(t)
 
         @when(j >= lowered)
@@ -413,7 +420,7 @@
     rows_dev, cols_dev = matrix.shape
     block = inverses.shape[1]
     kind = matrix.dtype
-    ny, nu, nr = rows_dev // SEND_ROWS, cols_dev // COL_CHUNK, rows_dev // ROW_CHUNK
+    ny, nu, nr = rows_dev // SEND_ROWS, U_HALVES * (cols_dev // COL_CHUNK), rows_dev // ROW_CHUNK
     dma = pltpu.SemaphoreType.DMA
     return pl.pallas_call(
         functools.partial(kernel, n_rows, n_cols),

time: 64.9 us -> 63.8 us (0.983)
  the two profiles are of different devices: /device:TPU:28 before, /device:TPU:31 now
where the time goes in v3:
time: 63.8 us; the launch traced here: 63.7 us
  Pallas kernels  59 us (92%)
  local copies, waits for them, and re-layouts  4.64 us (7%)
    pallas_call x1, Pallas kernels, per_device(): pl.pallas_call(functools.partial(kernel, n_rows, n_cols), out_shape=jax.S...  59 us
    unnamed x1, local copies, waits for them, and re-layouts  4.64 us

profile of v3, /device:TPU:31, one launch (start us, length us, event | category | flops | bytes accessed | tf_op | source)
XLA Modules:
  0.0 63.7 jit_solution(705873565202522921)
XLA Ops:
  0.0 59.0 %shard_map.28 = bf16[2048,1024]{1,0:T(8,128)(2,1)} custom-call(bf16[2048,1024]{1,0:T(8,128)(2,1)} %m.1, bf16[2,512,512]{2,1,0:T(8,128)(2,1)} %inv.1), custom_call_target="tpu_custom_call" | custom-call | tf_op jit(solution)/shard_map/pallas_call | solution.py:425
  59.0 4.6 %copy.4 = bf16[2048,1024]{1,0:T(8,128)(2,1)} copy(bf16[2048,1024]{1,0:T(8,128)(2,1)} %shard_map.28) | data formatting | bytes 8388608
